TPU v7x, 32 devices: a whole 2x2x4 slice. The times are simulated.
32 devices in a mesh: dp: 8 (over z, core), ctx: 4 (over y, x).
Axes of the slice: x: 2, y: 2, z: 4, core: 2. Of those that a mesh axis runs over, the one named last changes fastest.
Arguments:
- queries: bfloat16 [8, 1536, 1024], P('dp', 'ctx'), may hold values from -32 to 32
- keys: bfloat16 [8, 1536, 1024], P('dp', 'ctx'), may hold values from -32 to 32
- values: bfloat16 [8, 1536, 1024], P('dp', 'ctx'), may hold values from -6 to 6
- out_weight: bfloat16 [2048, 1024], replicated, may hold values from -0.1875 to 0.1875
- out_cot: bfloat16 [8, 1536, 2048], P('dp', 'ctx'), may hold values from -6 to 6
- block_list: int32 [12, 8], replicated, may hold values from 0 to 11, as said below
Outputs:
- attended: bfloat16 [8, 1536, 2048], P('dp', 'ctx')
- query_gradient: bfloat16 [8, 1536, 1024], P('dp', 'ctx')
- key_grad: bfloat16 [8, 1536, 1024], P('dp', 'ctx')
- value_grad: bfloat16 [8, 1536, 1024], P('dp', 'ctx')
- weight_grad: float32 [2048, 1024], P(('dp', 'ctx'))
Inputs may be any that keep to these rules, and one draw needn't show every extreme that they name: `block_list`: row i names 8 different blocks: i - 1, i and i + 1 modulo 12, then the 2 global blocks (the same in every row) where they are not among those three, then other blocks at random.
All inputs are finite; a program needn't handle non-finite values.
Results may differ from a plain program's by a relative error of at most 0.015.
Values may be sent and summed in bfloat16 or wider, within the bound.
A program may use at most 128 MiB of HBM per device.

v0:
```python
import functools
import math

import jax
import jax.numpy as jnp
from jax import lax
from jax.experimental import pallas as pl
from jax.experimental.pallas import tpu as pltpu
from jax.sharding import PartitionSpec as P

HEAD_SIZE = 128
BLOCK_TOKENS = 128
MESH = pl.DeviceIdType.MESH
BF16 = jnp.bfloat16
F32 = jnp.float32
VMEM_BYTES = 60 * 1024 * 1024


def mm(a, b, ca=1, cb=0):
    return lax.dot_general(a, b, (((ca,), (cb,)), ((), ())), preferred_element_type=F32)


def span(i, size):
    return pl.ds(pl.multiple_of(i * size, size), size)


def layer_kernel(n, nz, heads, names, picks, pos, q, k, v, w, oc, out, dqo, dko, dvo, wg, *scratch):
    r = dict(zip(names, scratch))
    me = lax.axis_index("ctx")
    dp = lax.axis_index("dp")
    core = lax.rem(dp, 2)
    other = dp + 1 - 2 * core
    z = dp // 2
    held = q.shape[0]
    tokens = held * BLOCK_TOKENS
    model = w.shape[0]
    blocks, chosen = picks.shape
    sub = wg.shape[0]
    scale = 1.0 / math.sqrt(HEAD_SIZE)
    factor = scale * math.log2(math.e)
    ocv, octv, wv, seq = r["ocv"], r["octv"], r["wv"], r["seq"]
    acc, ps, dss, kt, vt = r["acc"], r["ps"], r["dss"], r["kt"], r["vt"]
    loc = r["loc"]

    barrier = pltpu.get_barrier_semaphore()
    up = lax.rem(z + 1, nz) * 2 + core
    down = lax.rem(z + nz - 1, nz) * 2 + core
    for d in range(1, n):
        pl.semaphore_signal(
            barrier, inc=1, device_id=(dp, lax.rem(me + d, n)), device_id_type=MESH
        )
    for target in (other, up, down):
        pl.semaphore_signal(barrier, inc=1, device_id=(target, me), device_id_type=MESH)
    load_oc = pltpu.make_async_copy(oc, ocv, loc.at[0])
    load_oc.start()
    load_w = []
    for h in range(heads):
        for p in range(n):
            copy = pltpu.make_async_copy(
                w.at[:, pl.ds((p * heads + h) * HEAD_SIZE, HEAD_SIZE)],
                wv.at[h, :, pl.ds(p * HEAD_SIZE, HEAD_SIZE)],
                r["wsem"].at[h, p],
            )
            copy.start()
            load_w.append(copy)
    pl.semaphore_wait(barrier, n - 1 + 3)

    def trade(src_of, dst, send, recv, own_sem):
        remote = []
        for d in range(1, n):
            p = lax.rem(me + d, n)
            copy = pltpu.make_async_remote_copy(
                src_of(p, d), dst, send.at[d], recv.at[d],
                device_id=(dp, p), device_id_type=MESH,
            )
            copy.start()
            remote.append(copy)
        own = pltpu.make_async_copy(src_of(me, 0), dst, own_sem)
        own.start()
        return own, remote

    def column(p, h):
        return span(p * heads + h, HEAD_SIZE)

    mine = pl.ds(me * held, held)

    def send_rows(h):
        return [
            trade(
                lambda p, d, x=x: x.at[:, :, column(p, h)], r[f"{t}{h}"].at[mine],
                r["in_s"].at[h, i], r["in_r"].at[h, i], r["in_l"].at[h, i],
            )
            for i, (t, x) in enumerate((("q", q), ("k", k), ("v", v)))
        ]

    def send_cot(h):
        return [
            trade(
                lambda p, d: r["cotbuf"].at[h, d], r[f"c{h}"].at[mine],
                r["in_s"].at[h, 3], r["in_r"].at[h, 3], r["in_l"].at[h, 3],
            )
        ]

    def work_cot(h):
        for d in range(n):
            p = lax.rem(me + d, n)
            r["cotbuf"][h, d] = (
                mm(ocv[...], wv[h, :, span(p, HEAD_SIZE)])
                .astype(BF16)
                .reshape(held, BLOCK_TOKENS, HEAD_SIZE)
            )

    sent = []

    def arrive(trades):
        for own, remote in trades:
            own.wait()
            for copy in remote:
                copy.wait_recv()
            sent.extend(remote)

    coming = send_rows(0)
    load_oc.wait()
    for copy in load_w:
        copy.wait()
    work_cot(0)
    coming += send_cot(0)
    for h in range(1, heads):
        work_cot(h)

    def flip(i, carry):
        octv[span(i, 256), :] = ocv[:, span(i, 256)].T
        return carry

    lax.fori_loop(0, model // 256, flip, 0)

    def clear(i, carry):
        ps[i, chosen] = jnp.zeros((BLOCK_TOKENS, BLOCK_TOKENS), BF16)
        dss[i, chosen] = jnp.zeros((BLOCK_TOKENS, BLOCK_TOKENS), BF16)
        return carry

    lax.fori_loop(0, blocks, clear, 0)

    def attend(h, i):
        at = span(i, BLOCK_TOKENS)
        kh, vh = r[f"k{h}"], r[f"v{h}"]
        qi = r[f"q{h}"][i]
        ci = r[f"c{h}"][i]
        ids = [picks[i, j] for j in range(chosen)]
        ks = jnp.concatenate([kh[b] for b in ids], axis=0)
        vs = jnp.concatenate([vh[b] for b in ids], axis=0)
        kts = jnp.concatenate([kt[b] for b in ids], axis=1)
        vts = jnp.concatenate([vt[b] for b in ids], axis=1)
        st = mm(ks, qi, 1, 1)
        dpt = mm(vs, ci, 1, 1)
        top = jnp.max(st, axis=0, keepdims=True)
        e = jnp.exp2((st - top) * factor)
        inv = 1.0 / jnp.sum(e, axis=0, keepdims=True)
        pt = e * inv
        low = pt.astype(BF16)
        a = mm(vts, low).astype(BF16)
        r["attn"][h, at, :] = a.T
        dot = jnp.sum(ci.astype(F32).T * a.astype(F32), axis=0, keepdims=True)
        ds = (pt * (dpt - dot)).astype(BF16)
        r["dq"][h, at, :] = (mm(kts, ds) * scale).T.astype(BF16)
        for j in range(chosen):
            part = slice(j * BLOCK_TOKENS, (j + 1) * BLOCK_TOKENS)
            ps[i, j] = low[part]
            dss[i, j] = ds[part]

    group = math.gcd(blocks, 4)

    def collect(h):
        def wide(kept, g):
            return jnp.concatenate(
                [
                    jnp.concatenate([kept[i, pos[i, g * group + x]] for i in range(blocks)], axis=1)
                    for x in range(group)
                ],
                axis=0,
            )

        def body(g, carry):
            at = span(g, group * BLOCK_TOKENS)
            dst = wide(dss, g)
            r["dk"][h, at, :] = (mm(dst, r[f"q{h}"][...].reshape(-1, HEAD_SIZE)) * scale).astype(BF16)
            pst = wide(ps, g)
            r["dv"][h, at, :] = mm(pst, r[f"c{h}"][...].reshape(-1, HEAD_SIZE)).astype(BF16)
            return carry

        lax.fori_loop(0, blocks // group, body, 0)

    def turn(h):
        def body(b, carry):
            kt[b] = r[f"k{h}"][b].T
            vt[b] = r[f"v{h}"][b].T
            return carry

        lax.fori_loop(0, blocks, body, 0)

    def send_attn(h):
        return [
            trade(
                lambda p, d: r["attn"].at[h, span(p, tokens), :],
                seq.at[h, :, span(me, HEAD_SIZE)],
                r["out_s"].at[h, 0], r["out_r"].at[h, 0], r["out_l"].at[h, 0],
            )
        ]

    def send_grads(h):
        return [
            trade(
                lambda p, d, t=t: r[t].at[h, span(p, tokens), :], o.at[:, column(me, h)],
                r["out_s"].at[h, i], r["out_r"].at[h, i], r["out_l"].at[h, i],
            )
            for i, t, o in ((1, "dq", dqo), (2, "dk", dko), (3, "dv", dvo))
        ]

    def term(h, c, who):
        return mm(octv[span(2 * c + who, n * sub), :], seq[h]).reshape(n, sub, -1)

    def core_copy(h, c):
        return pltpu.make_async_remote_copy(
            r["csend"].at[h, c], r["crecv"].at[h, c], r["csem_s"].at[h, c], r["csem_r"].at[h, c],
            device_id=(other, me), device_id_type=MESH,
        )

    def give(h):
        def body(c, carry):
            r["csend"][h, c] = term(h, c, 1 - core).astype(BF16)
            core_copy(h, c).start()
            return carry

        lax.fori_loop(0, nz, body, 0)

        def keep(c, carry):
            acc[h, c] = term(h, c, core)
            return carry

        lax.fori_loop(0, nz, keep, 0)

    def take(h):
        def body(c, carry):
            core_copy(h, c).wait()
            for s in range(n):
                acc[h, c, s] += r["crecv"][h, c, s].astype(F32)
            return carry

        lax.fori_loop(0, nz, body, 0)

    def hop(h, c, s, buf, sem, target):
        return pltpu.make_async_remote_copy(
            r["zsend"].at[h, c, s], r[buf].at[h, c, s], r["zsem"].at[h, c, s],
            r[sem].at[h, c, s], device_id=(target, me), device_id_type=MESH,
        )

    def right(h, c, s):
        return hop(h, c, s, "rrecv", "rsem", up)

    def left(h, c, s):
        return hop(h, c, s, "lrecv", "lsem", down)

    def line(h, u):
        i = u - z

        @pl.when((i >= 0) & (i < (nz - 1 - z) * n))
        def _():
            c = nz - 1 - i // n
            s = lax.rem(i, n)

            @pl.when(z > 0)
            def _():
                right(h, c, s).wait_recv()
                acc[h, c, s] += r["rrecv"][h, c, s].astype(F32)

            r["zsend"][h, c, s] = acc[h, c, s].astype(BF16)
            right(h, c, s).start()

        j = u - (nz - 1 - z)

        @pl.when((j >= 0) & (j < z * n))
        def _():
            c = j // n
            s = lax.rem(j, n)

            @pl.when(z < nz - 1)
            def _():
                left(h, c, s).wait_recv()
                acc[h, c, s] += r["lrecv"][h, c, s].astype(F32)

            r["zsend"][h, c, s] = acc[h, c, s].astype(BF16)
            left(h, c, s).start()

    hops = (nz - 1) * n + nz

    def lines(h, first):
        def body(u, carry):
            line(h, u)
            return carry

        lax.fori_loop(first, hops, body, 0)

    def cross(h, s, slot):
        return pltpu.make_async_remote_copy(
            r["xsend"].at[h, s], r["xrecv"].at[h, slot], r["xsem_s"].at[h, s],
            r["xsem_r"].at[h, slot], device_id=(dp, s), device_id_type=MESH,
        )

    def finish(h):
        def body(s, carry):
            @pl.when(z > 0)
            def _():
                right(h, z, s).wait_recv()
                acc[h, z, s] += r["rrecv"][h, z, s].astype(F32)

            @pl.when(z < nz - 1)
            def _():
                left(h, z, s).wait_recv()
                acc[h, z, s] += r["lrecv"][h, z, s].astype(F32)

            @pl.when(s != me)
            def _():
                r["xsend"][h, s] = acc[h, z, s].astype(BF16)
                cross(h, s, me).start()

            return carry

        lax.fori_loop(0, n, body, 0)

    def total(h):
        r["sum"][...] = acc[h, z, me]

        def body(p, carry):
            @pl.when(p != me)
            def _():
                cross(h, p, p).wait_recv()
                r["sum"][...] += r["xrecv"][h, p].astype(F32)

            return carry

        lax.fori_loop(0, n, body, 0)
        for p in range(n):
            wg[:, pl.ds((p * heads + h) * HEAD_SIZE, HEAD_SIZE)] = r["sum"][
                :, p * HEAD_SIZE : (p + 1) * HEAD_SIZE
            ] * (1.0 / (2 * nz))

    def drain(h):
        def body(s, carry):
            @pl.when(s != me)
            def _():
                cross(h, s, me).wait_send()

            for c in range(nz):
                @pl.when(z < c)
                def _():
                    right(h, c, s).wait_send()

                @pl.when(z > c)
                def _():
                    left(h, c, s).wait_send()

            return carry

        lax.fori_loop(0, n, body, 0)

    pair = math.gcd(blocks, 2)
    turns = blocks // pair
    begin = turns // 2
    per = 3
    done = min(hops, (turns - begin) * per)
    going, attn_going = [], []
    for h in range(heads):
        arrive(coming)
        if h + 1 < heads:
            coming = send_rows(h + 1) + send_cot(h + 1)
        turn(h)

        def body(t, carry, h=h):
            for b in range(pair):
                attend(h, t * pair + b)
            if h > 0:
                @pl.when(t == begin - 1)
                def _():
                    give(h - 1)

                @pl.when(t == begin)
                def _():
                    take(h - 1)

                @pl.when(t >= begin)
                def _():
                    for x in range(per):
                        line(h - 1, (t - begin) * per + x)

            return carry

        if h > 0:
            split = min(begin - 1, 2)
            lax.fori_loop(0, split, body, 0)
            arrive(attn_going)
            lax.fori_loop(split, turns, body, 0)
        else:
            lax.fori_loop(0, turns, body, 0)
        attn_going = send_attn(h)
        collect(h)
        if h > 0:
            lines(h - 1, done)
            finish(h - 1)
        if h + 1 < heads:
            going += send_grads(h)
    arrive(attn_going)
    going += send_grads(heads - 1)
    give(heads - 1)
    tile = 256

    def project(i, carry):
        at = span(i, tile)
        part = mm(seq[0], wv[0, at, :], 1, 1)
        for h in range(1, heads):
            part += mm(seq[h], wv[h, at, :], 1, 1)
        out[:, at] = part.astype(BF16)
        return carry

    take(heads - 1)

    def both(u, carry):
        line(heads - 1, u)

        @pl.when(u < model // tile)
        def _():
            project(u, 0)

        return carry

    lax.fori_loop(0, max(hops, model // tile), both, 0)
    finish(heads - 1)
    for h in range(heads):
        total(h)
    for h in range(heads):
        drain(h)
    arrive(going)
    for copy in sent:
        copy.wait_send()


def shards(queries, keys, values, out_weight, out_cot, block_list):
    n = lax.axis_size("ctx")
    n_dp = lax.axis_size("dp")
    nz = n_dp // 2
    _, tokens, total = queries.shape
    model = out_weight.shape[0]
    heads = total // n // HEAD_SIZE
    length = tokens * n
    held = tokens // BLOCK_TOKENS
    blocks, chosen = block_list.shape
    sub = model // (n * n_dp)
    anyspec = pl.BlockSpec(memory_space=pl.ANY)
    vspec = pl.BlockSpec(memory_space=pltpu.VMEM)
    sspec = pl.BlockSpec(memory_space=pltpu.SMEM)
    dma = pltpu.SemaphoreType.DMA

    listed = block_list[:, :, None] == jnp.arange(blocks, dtype=jnp.int32)
    slot = jnp.arange(chosen, dtype=jnp.int32)[None, :, None] - chosen
    pos = chosen + jnp.sum(jnp.where(listed, slot, 0), axis=1)

    width = n * HEAD_SIZE
    lane = (heads, nz, n, sub, width)
    cross = (heads, n, sub, width)
    byhead = (heads, length, HEAD_SIZE)
    scratch = {
        "ocv": pltpu.VMEM((tokens, model), BF16),
        "octv": pltpu.VMEM((model, tokens), BF16),
        "wv": pltpu.VMEM((heads, model, width), BF16),
        "seq": pltpu.VMEM((heads, tokens, width), BF16),
        "cotbuf": pltpu.VMEM((heads, n, held, BLOCK_TOKENS, HEAD_SIZE), BF16),
        "attn": pltpu.VMEM(byhead, BF16),
        "dq": pltpu.VMEM(byhead, BF16),
        "dk": pltpu.VMEM(byhead, BF16),
        "dv": pltpu.VMEM(byhead, BF16),
        "ps": pltpu.VMEM((blocks, chosen + 1, BLOCK_TOKENS, BLOCK_TOKENS), BF16),
        "dss": pltpu.VMEM((blocks, chosen + 1, BLOCK_TOKENS, BLOCK_TOKENS), BF16),
        "kt": pltpu.VMEM((blocks, HEAD_SIZE, BLOCK_TOKENS), BF16),
        "vt": pltpu.VMEM((blocks, HEAD_SIZE, BLOCK_TOKENS), BF16),
        "acc": pltpu.VMEM(lane, F32),
        "sum": pltpu.VMEM((sub, width), F32),
        "csend": pltpu.VMEM(lane, BF16),
        "crecv": pltpu.VMEM(lane, BF16),
        "zsend": pltpu.VMEM(lane, BF16),
        "rrecv": pltpu.VMEM(lane, BF16),
        "lrecv": pltpu.VMEM(lane, BF16),
        "xsend": pltpu.VMEM(cross, BF16),
        "xrecv": pltpu.VMEM(cross, BF16),
        "loc": dma((1,)),
        "wsem": dma((heads, n)),
        "in_s": dma((heads, 4, n)),
        "in_r": dma((heads, 4, n)),
        "in_l": dma((heads, 4)),
        "out_s": dma((heads, 4, n)),
        "out_r": dma((heads, 4, n)),
        "out_l": dma((heads, 4)),
        "csem_s": dma((heads, nz)),
        "csem_r": dma((heads, nz)),
        "zsem": dma((heads, nz, n)),
        "rsem": dma((heads, nz, n)),
        "lsem": dma((heads, nz, n)),
        "xsem_s": dma((heads, n)),
        "xsem_r": dma((heads, n)),
    }
    for h in range(heads):
        for t in "qkvc":
            scratch[f"{t}{h}"] = pltpu.VMEM((blocks, BLOCK_TOKENS, HEAD_SIZE), BF16)
    rows = [x.reshape(held, BLOCK_TOKENS, total) for x in (queries, keys, values)]
    bytoken = jax.ShapeDtypeStruct((tokens, total), BF16)
    out, dq, dk, dv, wg = pl.pallas_call(
        functools.partial(layer_kernel, n, nz, heads, tuple(scratch)),
        out_shape=(
            jax.ShapeDtypeStruct((tokens, model), BF16),
            bytoken,
            bytoken,
            bytoken,
            jax.ShapeDtypeStruct((sub, total), F32),
        ),
        in_specs=[sspec] * 2 + [anyspec] * 5,
        out_specs=(vspec, anyspec, anyspec, anyspec, vspec),
        scratch_shapes=list(scratch.values()),
        compiler_params=pltpu.CompilerParams(
            collective_id=0, has_side_effects=True, vmem_limit_bytes=VMEM_BYTES
        ),
    )(block_list, pos, *rows, out_weight, out_cot[0])
    return out[None], dq[None], dk[None], dv[None], wg


def solution(mesh):
    part = P("dp", "ctx", None)
    return jax.shard_map(
        shards,
        mesh=mesh,
        in_specs=(part, part, part, P(), part, P()),
        out_specs=(part, part, part, part, P(("dp", "ctx"), None)),
        check_vma=False,
    )
```

profile of v0, /device:TPU:8, one launch (start us, length us, event | category | flops | bytes accessed | tf_op | source)
XLA Modules:
  0.0 115.4 jit_solution(2014867263521158485)
XLA Ops:
  0.6 0.8 copy.14.picks
  1.4 0.0 copy-start.4
  1.4 0.1 select_reduce_fusion
  1.5 0.6 broadcast_add_fusion.pos
  2.1 0.0 copy-done.4
  2.1 106.6 %shard_map.101 = (bf16[384,2048]{1,0:T(8,128)(2,1)}, bf16[384,1024]{1,0:T(8,128)(2,1)}, bf16[384,1024]{1,0:T(8,128)(2,1)}, bf16[384,1024]{1,0:T(8,128)(2,1)}, f32[64,1024]{1,0:T(8,128)}) custom-call(s32[12,8]{1,0:T(8,128)} %copy-done.4, s32[12,12]{1,0:T(8,128)} %broadcast_add_fusion.pos, bf16[3,128,1024]{2,1,0:T(8,128)(2,1)} %bitcast.13, ...), custom_call_target="tpu_custom_call" | custom-call | tf_op jit(solution)/shard_map/pallas_call | solution.py:514
  108.7 0.0 copy-start.2
  108.7 2.8 %copy.20 = bf16[1,384,2048]{2,1,0:T(8,128)(2,1)} copy(bf16[1,384,2048]{2,1,0:T(8,128)(2,1)} %bitcast.8) | data formatting | bytes 3145728
  111.5 0.0 copy-done.2
  111.5 0.0 copy-start.1
  111.5 0.0 copy-start
  111.6 0.9 copy.21
  112.4 0.5 copy-done.1
  113.0 0.0 copy-start.3
  113.0 0.9 copy.22
  113.8 0.0 copy-done
  113.8 0.9 copy.23
  114.7 0.0 copy-done.3
  114.7 0.7 copy.24
  (1 shorter events, 0.0 us)
Async XLA Ops:
  1.4 0.7 copy-start.4
  108.7 2.8 %copy-start.2 = (bf16[384,1024]{1,0:T(8,128)(2,1)S(1)}, bf16[384,1024]{1,0:T(8,128)(2,1)}, u32[]{:S(2)}) copy-start(bf16[384,1024]{1,0:T(8,128)(2,1)} %get-tuple-element.11) | copy-start | bytes 2359300
  111.5 1.4 %copy-start.1 = (bf16[384,1024]{1,0:T(8,128)(2,1)S(1)}, bf16[384,1024]{1,0:T(8,128)(2,1)}, u32[]{:S(2)}) copy-start(bf16[384,1024]{1,0:T(8,128)(2,1)} %get-tuple-element.12) | copy-start | bytes 2359300
  111.5 2.3 %copy-start = (bf16[384,1024]{1,0:T(8,128)(2,1)S(1)}, bf16[384,1024]{1,0:T(8,128)(2,1)}, u32[]{:S(2)}) copy-start(bf16[384,1024]{1,0:T(8,128)(2,1)} %get-tuple-element.13) | copy-start | bytes 2359300
  113.0 1.8 %copy-start.3 = (f32[64,1024]{1,0:T(8,128)S(1)}, f32[64,1024]{1,0:T(8,128)}, u32[]{:S(2)}) copy-start(f32[64,1024]{1,0:T(8,128)} %get-tuple-element.24) | copy-start | bytes 786436
where the time goes:
time: 116 us; the launch traced here: 115 us
  Pallas kernels  107 us (92%)
  local copies, waits for them, and re-layouts  7.46 us (6%)
    pallas_call x1, Pallas kernels, shards(): pl.pallas_call(functools.partial(layer_kernel, n, nz, heads, tuple(scratc...  107 us
    unnamed x16, local copies, waits for them, and re-layouts  7.46 us

commit v1 on v0

v1 whole, which is shorter than its diff:
```python
import functools
import math

import jax
import jax.numpy as jnp
from jax import lax
from jax.experimental import pallas as pl
from jax.experimental.pallas import tpu as pltpu
from jax.sharding import PartitionSpec as P

HEAD_SIZE = 128
BLOCK_TOKENS = 128
MESH = pl.DeviceIdType.MESH
BF16 = jnp.bfloat16
F32 = jnp.float32
VMEM_BYTES = 60 * 1024 * 1024


def mm(a, b, ca=1, cb=0):
    return lax.dot_general(a, b, (((ca,), (cb,)), ((), ())), preferred_element_type=F32)


def span(i, size):
    return pl.ds(pl.multiple_of(i * size, size), size)


def layer_kernel(n, nz, heads, names, picks, q, k, v, w, oc, out, dqo, dko, dvo, wg, *scratch):
    r = dict(zip(names, scratch))
    me = lax.axis_index("ctx")
    dp = lax.axis_index("dp")
    core = lax.rem(dp, 2)
    other = dp + 1 - 2 * core
    z = dp // 2
    held = q.shape[0]
    tokens = held * BLOCK_TOKENS
    model = w.shape[0]
    chosen, blocks = picks.shape
    sub = wg.shape[0]
    empty = blocks * chosen
    scale = 1.0 / math.sqrt(HEAD_SIZE)
    factor = scale * math.log2(math.e)
    ocv, octv, wv, seq = r["ocv"], r["octv"], r["wv"], r["seq"]
    acc, ps, dss, kt, vt = r["acc"], r["ps"], r["dss"], r["kt"], r["vt"]
    pos, loc = r["pos"], r["loc"]

    barrier = pltpu.get_barrier_semaphore()
    up = lax.rem(z + 1, nz) * 2 + core
    down = lax.rem(z + nz - 1, nz) * 2 + core
    for d in range(1, n):
        pl.semaphore_signal(
            barrier, inc=1, device_id=(dp, lax.rem(me + d, n)), device_id_type=MESH
        )
    for target in (other, up, down):
        pl.semaphore_signal(barrier, inc=1, device_id=(target, me), device_id_type=MESH)
    pl.semaphore_wait(barrier, n - 1 + 3)

    def partner(d):
        return lax.rem(me + d, n)

    def column(p, h):
        return span(p * heads + h, HEAD_SIZE)

    mine = pl.ds(me * held, held)

    class Trade:
        def __init__(self, src_of, dst, sems, where):
            self.src_of, self.dst = src_of, dst
            self.send, self.recv, self.own_sem = (r[sems + x].at[where] for x in "srl")

        def copy(self, d):
            p = partner(d)
            return pltpu.make_async_remote_copy(
                self.src_of(p), self.dst, self.send.at[d], self.recv.at[d],
                device_id=(dp, p), device_id_type=MESH,
            )

        def own(self):
            return pltpu.make_async_copy(self.src_of(me), self.dst, self.own_sem)

        def start(self):
            for d in range(1, n):
                self.copy(d).start()
            self.own().start()

        def arrive(self):
            self.own().wait()
            for d in range(1, n):
                self.copy(d).wait_recv()

        def sent(self):
            for d in range(1, n):
                self.copy(d).wait_send()

    rows = {
        (t, h): Trade(lambda p, x=x, h=h: x.at[:, :, column(p, h)], r[f"{t}{h}"].at[mine], "in_", (h, i))
        for i, (t, x) in enumerate((("k", k), ("q", q), ("v", v)))
        for h in range(heads)
    }
    cots = [
        Trade(lambda p, h=h: r["cotbuf"].at[h, p], r[f"c{h}"].at[mine], "in_", (h, 3))
        for h in range(heads)
    ]
    attns = [
        Trade(
            lambda p, h=h: r["attn"].at[h, span(p, tokens), :],
            seq.at[h, :, span(me, HEAD_SIZE)], "out_", (h, 0),
        )
        for h in range(heads)
    ]
    grads = {
        (t, h): Trade(
            lambda p, h=h, t=t: r[t].at[h, span(p, tokens), :], o.at[:, column(me, h)], "out_", (h, i)
        )
        for i, t, o in ((1, "dq", dqo), (2, "dk", dko), (3, "dv", dvo))
        for h in range(heads)
    }

    for h in range(heads):
        for t in "kqv":
            rows[t, h].start()
    load_oc = pltpu.make_async_copy(oc, ocv, loc.at[0])
    load_oc.start()
    load_w = []
    for h in range(heads):
        for p in range(n):
            copy = pltpu.make_async_copy(
                w.at[:, pl.ds((p * heads + h) * HEAD_SIZE, HEAD_SIZE)],
                wv.at[h, :, pl.ds(p * HEAD_SIZE, HEAD_SIZE)],
                r["wsem"].at[h, p],
            )
            copy.start()
            load_w.append(copy)

    def place(i, carry):
        def one(b, carry):
            at = empty
            for j in range(chosen):
                at = jnp.where(picks[j, i] == b, i * chosen + j, at)
            pos[i, b] = at
            return carry

        return lax.fori_loop(0, blocks, one, carry)

    lax.fori_loop(0, blocks, place, 0)
    for h in range(heads):
        ps[h, empty] = jnp.zeros((BLOCK_TOKENS, BLOCK_TOKENS), BF16)
    dss[empty] = jnp.zeros((BLOCK_TOKENS, BLOCK_TOKENS), BF16)

    load_oc.wait()

    def flip(i, carry):
        octv[span(i, 256), :] = ocv[:, span(i, 256)].T
        return carry

    lax.fori_loop(0, model // 256, flip, 0)
    for copy in load_w:
        copy.wait()

    def work_cot(h):
        def body(p, carry):
            r["cotbuf"][h, p] = (
                mm(ocv[...], wv[h, :, span(p, HEAD_SIZE)])
                .astype(BF16)
                .reshape(held, BLOCK_TOKENS, HEAD_SIZE)
            )
            return carry

        lax.fori_loop(0, n, body, 0)

    for h in range(heads):
        work_cot(h)

    def listed(ref, i, axis):
        return jnp.concatenate([ref[picks[j, i]] for j in range(chosen)], axis=axis)

    def forward_block(h, i):
        st = mm(listed(r[f"k{h}"], i, 0), r[f"q{h}"][i], 1, 1)
        top = jnp.max(st, axis=0, keepdims=True)
        e = jnp.exp2((st - top) * factor)
        inv = 1.0 / jnp.sum(e, axis=0, keepdims=True)
        low = (e * inv).astype(BF16)
        a = mm(listed(vt, i, 1), low).astype(BF16)
        r["attn"][h, span(i, BLOCK_TOKENS), :] = a.T
        for j in range(chosen):
            ps[h, i * chosen + j] = low[j * BLOCK_TOKENS : (j + 1) * BLOCK_TOKENS]

    def backward_block(h, i):
        at = span(i, BLOCK_TOKENS)
        ci = r[f"c{h}"][i]
        dpt = mm(listed(r[f"v{h}"], i, 0), ci, 1, 1)
        dot = jnp.sum(
            (ci.astype(F32) * r["attn"][h, at, :].astype(F32)).T, axis=0, keepdims=True
        )
        parts = []
        for j in range(chosen):
            part = slice(j * BLOCK_TOKENS, (j + 1) * BLOCK_TOKENS)
            ds = (ps[h, i * chosen + j].astype(F32) * (dpt[part] - dot)).astype(BF16)
            dss[i * chosen + j] = ds
            parts.append(ds)
        r["dq"][h, at, :] = (mm(listed(kt, i, 1), jnp.concatenate(parts, axis=0)) * scale).T.astype(BF16)

    def collect_part(h, p):
        def wide(kept):
            return jnp.concatenate(
                [
                    jnp.concatenate([kept(pos[i, p * held + x]) for i in range(blocks)], axis=1)
                    for x in range(held)
                ],
                axis=0,
            )

        at = span(p, tokens)
        pst = wide(lambda slot: ps[h, slot])
        r["dv"][h, at, :] = mm(pst, r[f"c{h}"][...].reshape(-1, HEAD_SIZE)).astype(BF16)
        dst = wide(lambda slot: dss[slot])
        r["dk"][h, at, :] = (mm(dst, r[f"q{h}"][...].reshape(-1, HEAD_SIZE)) * scale).astype(BF16)

    def turn(src, dst):
        def body(b, carry):
            dst[b] = src[b].T
            return carry

        lax.fori_loop(0, blocks, body, 0)

    def by_partner(work, trades, hooks):
        def body(t, carry):
            d = t + 1
            work(partner(d))

            @pl.when(d < n)
            def _():
                for trade in trades:
                    trade.copy(d).start()

            for at, hook in hooks.items():
                pl.when(t == at)(hook)
            return carry

        lax.fori_loop(0, n, body, 0)
        for trade in trades:
            trade.own().start()

    def forward(h):
        for t in "kqv":
            rows[t, h].arrive()
        turn(r[f"v{h}"], vt)

        def work(p):
            for x in range(held):
                forward_block(h, p * held + x)

        by_partner(work, [attns[h]], {})

    def backward(h, hooks):
        turn(r[f"k{h}"], kt)
        cots[h].arrive()

        def work(p):
            for x in range(held):
                backward_block(h, p * held + x)

        by_partner(work, [grads["dq", h]], hooks)

    def collect(h, hooks):
        by_partner(lambda p: collect_part(h, p), [grads["dv", h], grads["dk", h]], hooks)

    def term(h, c, who):
        return mm(octv[span(2 * c + who, n * sub), :], seq[h]).reshape(n, sub, -1)

    def core_copy(h, c):
        return pltpu.make_async_remote_copy(
            r["csend"].at[h, c], r["crecv"].at[h, c], r["csem_s"].at[h, c], r["csem_r"].at[h, c],
            device_id=(other, me), device_id_type=MESH,
        )

    def give(h):
        def body(c, carry):
            r["csend"][h, c] = term(h, c, 1 - core).astype(BF16)
            core_copy(h, c).start()
            return carry

        lax.fori_loop(0, nz, body, 0)

        def keep(c, carry):
            acc[h, c] = term(h, c, core)
            return carry

        lax.fori_loop(0, nz, keep, 0)

    def take(h):
        def body(c, carry):
            core_copy(h, c).wait()
            for s in range(n):
                acc[h, c, s] += r["crecv"][h, c, s].astype(F32)
            return carry

        lax.fori_loop(0, nz, body, 0)

    def hop(h, c, s, buf, sem, target):
        return pltpu.make_async_remote_copy(
            r["zsend"].at[h, c, s], r[buf].at[h, c, s], r["zsem"].at[h, c, s],
            r[sem].at[h, c, s], device_id=(target, me), device_id_type=MESH,
        )

    def right(h, c, s):
        return hop(h, c, s, "rrecv", "rsem", up)

    def left(h, c, s):
        return hop(h, c, s, "lrecv", "lsem", down)

    def burst(h, b):
        def one_way(rank, chunk_of, link, buf):
            count = jnp.where(rank == 0, nz - 1 if b == 0 else 0, jnp.where(rank <= b, 1, 0))

            def body(i, carry):
                c = chunk_of(b - rank + i // n)
                s = lax.rem(i, n)

                @pl.when(rank > 0)
                def _():
                    link(h, c, s).wait_recv()
                    acc[h, c, s] += r[buf][h, c, s].astype(F32)

                r["zsend"][h, c, s] = acc[h, c, s].astype(BF16)
                link(h, c, s).start()
                return carry

            lax.fori_loop(0, count * n, body, 0)

        one_way(z, lambda x: nz - 1 - x, right, "rrecv")
        one_way(nz - 1 - z, lambda x: x, left, "lrecv")

    def cross(h, s, slot):
        return pltpu.make_async_remote_copy(
            r["xsend"].at[h, s], r["xrecv"].at[h, slot], r["xsem_s"].at[h, s],
            r["xsem_r"].at[h, slot], device_id=(dp, s), device_id_type=MESH,
        )

    def finish(h):
        def body(s, carry):
            @pl.when(z > 0)
            def _():
                right(h, z, s).wait_recv()
                acc[h, z, s] += r["rrecv"][h, z, s].astype(F32)

            @pl.when(z < nz - 1)
            def _():
                left(h, z, s).wait_recv()
                acc[h, z, s] += r["lrecv"][h, z, s].astype(F32)

            @pl.when(s != me)
            def _():
                r["xsend"][h, s] = acc[h, z, s].astype(BF16)
                cross(h, s, me).start()

            return carry

        lax.fori_loop(0, n, body, 0)

    def total(h):
        r["sum"][...] = acc[h, z, me]

        def body(p, carry):
            @pl.when(p != me)
            def _():
                cross(h, p, p).wait_recv()
                r["sum"][...] += r["xrecv"][h, p].astype(F32)

            return carry

        lax.fori_loop(0, n, body, 0)
        for p in range(n):
            wg[:, pl.ds((p * heads + h) * HEAD_SIZE, HEAD_SIZE)] = r["sum"][
                :, p * HEAD_SIZE : (p + 1) * HEAD_SIZE
            ] * (1.0 / (2 * nz))

    def drain(h):
        def body(s, carry):
            @pl.when(s != me)
            def _():
                cross(h, s, me).wait_send()

            for c in range(nz):
                @pl.when(z < c)
                def _():
                    right(h, c, s).wait_send()

                @pl.when(z > c)
                def _():
                    left(h, c, s).wait_send()

            return carry

        lax.fori_loop(0, n, body, 0)

    tile = 256
    store = pltpu.make_async_copy(r["outv"], out, loc.at[1])

    def project():
        def body(i, carry):
            at = span(i, tile)
            part = mm(seq[0], wv[0, at, :], 1, 1)
            for h in range(1, heads):
                part += mm(seq[h], wv[h, at, :], 1, 1)
            r["outv"][:, at] = part.astype(BF16)
            return carry

        lax.fori_loop(0, model // tile, body, 0)
        store.start()

    for h in range(heads):
        forward(h)
        cots[h].start()
    for h in range(heads):
        attns[h].arrive()
        give(h)
        take(h)
        burst(h, 0)
        hooks = {n // 2 - 1: lambda: burst(h, 1)}
        if h > 0:
            hooks[0] = lambda: finish(h - 1)
        backward(h, hooks)
        collect(h, {n // 2 - 1: lambda: burst(h, 2)})
        for b in range(3, nz - 1):
            burst(h, b)
    project()
    finish(heads - 1)
    for h in range(heads):
        total(h)
    for h in range(heads):
        drain(h)
    for trade in grads.values():
        trade.arrive()
    for trade in (*rows.values(), *cots, *attns, *grads.values()):
        trade.sent()
    store.wait()


def shards(queries, keys, values, out_weight, out_cot, block_list):
    n = lax.axis_size("ctx")
    n_dp = lax.axis_size("dp")
    nz = n_dp // 2
    _, tokens, total = queries.shape
    model = out_weight.shape[0]
    heads = total // n // HEAD_SIZE
    length = tokens * n
    held = tokens // BLOCK_TOKENS
    blocks, chosen = block_list.shape
    sub = model // (n * n_dp)
    anyspec = pl.BlockSpec(memory_space=pl.ANY)
    vspec = pl.BlockSpec(memory_space=pltpu.VMEM)
    sspec = pl.BlockSpec(memory_space=pltpu.SMEM)
    dma = pltpu.SemaphoreType.DMA

    width = n * HEAD_SIZE
    lane = (heads, nz, n, sub, width)
    cross = (heads, n, sub, width)
    byhead = (heads, length, HEAD_SIZE)
    scratch = {
        "ocv": pltpu.VMEM((tokens, model), BF16),
        "octv": pltpu.VMEM((model, tokens), BF16),
        "wv": pltpu.VMEM((heads, model, width), BF16),
        "seq": pltpu.VMEM((heads, tokens, width), BF16),
        "outv": pltpu.VMEM((tokens, model), BF16),
        "cotbuf": pltpu.VMEM((heads, n, held, BLOCK_TOKENS, HEAD_SIZE), BF16),
        "attn": pltpu.VMEM(byhead, BF16),
        "dq": pltpu.VMEM(byhead, BF16),
        "dk": pltpu.VMEM(byhead, BF16),
        "dv": pltpu.VMEM(byhead, BF16),
        "ps": pltpu.VMEM((heads, blocks * chosen + 1, BLOCK_TOKENS, BLOCK_TOKENS), BF16),
        "dss": pltpu.VMEM((blocks * chosen + 1, BLOCK_TOKENS, BLOCK_TOKENS), BF16),
        "kt": pltpu.VMEM((blocks, HEAD_SIZE, BLOCK_TOKENS), BF16),
        "vt": pltpu.VMEM((blocks, HEAD_SIZE, BLOCK_TOKENS), BF16),
        "acc": pltpu.VMEM(lane, F32),
        "sum": pltpu.VMEM((sub, width), F32),
        "csend": pltpu.VMEM(lane, BF16),
        "crecv": pltpu.VMEM(lane, BF16),
        "zsend": pltpu.VMEM(lane, BF16),
        "rrecv": pltpu.VMEM(lane, BF16),
        "lrecv": pltpu.VMEM(lane, BF16),
        "xsend": pltpu.VMEM(cross, BF16),
        "xrecv": pltpu.VMEM(cross, BF16),
        "pos": pltpu.SMEM((blocks, blocks), jnp.int32),
        "loc": dma((2,)),
        "wsem": dma((heads, n)),
        "in_s": dma((heads, 4, n)),
        "in_r": dma((heads, 4, n)),
        "in_l": dma((heads, 4)),
        "out_s": dma((heads, 4, n)),
        "out_r": dma((heads, 4, n)),
        "out_l": dma((heads, 4)),
        "csem_s": dma((heads, nz)),
        "csem_r": dma((heads, nz)),
        "zsem": dma((heads, nz, n)),
        "rsem": dma((heads, nz, n)),
        "lsem": dma((heads, nz, n)),
        "xsem_s": dma((heads, n)),
        "xsem_r": dma((heads, n)),
    }
    for h in range(heads):
        for t in "qkvc":
            scratch[f"{t}{h}"] = pltpu.VMEM((blocks, BLOCK_TOKENS, HEAD_SIZE), BF16)
    rows = [x.reshape(held, BLOCK_TOKENS, total) for x in (queries, keys, values)]
    bytoken = jax.ShapeDtypeStruct((tokens, total), BF16)
    out, dq, dk, dv, wg = pl.pallas_call(
        functools.partial(layer_kernel, n, nz, heads, tuple(scratch)),
        out_shape=(
            jax.ShapeDtypeStruct((tokens, model), BF16),
            bytoken,
            bytoken,
            bytoken,
            jax.ShapeDtypeStruct((sub, total), F32),
        ),
        in_specs=[sspec] + [anyspec] * 5,
        out_specs=(anyspec, anyspec, anyspec, anyspec, vspec),
        scratch_shapes=list(scratch.values()),
        compiler_params=pltpu.CompilerParams(
            collective_id=0, has_side_effects=True, vmem_limit_bytes=VMEM_BYTES
        ),
    )(block_list.T, *rows, out_weight, out_cot[0])
    return out[None], dq[None], dk[None], dv[None], wg


def solution(mesh):
    part = P("dp", "ctx", None)
    return jax.shard_map(
        shards,
        mesh=mesh,
        in_specs=(part, part, part, P(), part, P()),
        out_specs=(part, part, part, part, P(("dp", "ctx"), None)),
        check_vma=False,
    )
```

time: 116 us -> 95.2 us (0.82)
  Pallas kernels: 107 us -> 87.1 us
  local copies, waits for them, and re-layouts: 7.46 us -> 6.2 us
    pallas_call x1, Pallas kernels: 107 us -> 87.1 us  [shards(): pl.pallas_call(functools.partial(layer_kernel, n, nz, heads, tuple(scratc...]
    unnamed x16 -> x13, local copies, waits for them, and re-layouts: 7.46 us -> 6.2 us
where the time goes in v1:
time: 95.2 us; the launch traced here: 94 us
  Pallas kernels  87.1 us (91%)
  local copies, waits for them, and re-layouts  6.2 us (7%)
    pallas_call x1, Pallas kernels, shards(): pl.pallas_call(functools.partial(layer_kernel, n, nz, heads, tuple(scratc...  87.1 us
    unnamed x13, local copies, waits for them, and re-layouts  6.2 us

profile of v1, /device:TPU:8, one launch (start us, length us, event | category | flops | bytes accessed | tf_op | source)
XLA Modules:
  0.0 94.0 jit_solution(14188041392157663469)
XLA Ops:
  0.6 87.1 %shard_map.101 = (bf16[384,2048]{1,0:T(8,128)(2,1)}, bf16[384,1024]{1,0:T(8,128)(2,1)}, bf16[384,1024]{1,0:T(8,128)(2,1)}, bf16[384,1024]{1,0:T(8,128)(2,1)}, f32[64,1024]{1,0:T(8,128)}) custom-call(s32[8,12]{1,0:T(8,128)} %bitcast.17, bf16[3,128,1024]{2,1,0:T(8,128)(2,1)} %bitcast.11, bf16[3,128,1024]{2,1,0:T(8,128)(2,1)} %bitcast.12, ...), custom_call_target="tpu_custom_call" | custom-call | tf_op jit(solution)/shard_map/pallas_call | solution.py:505
  87.8 0.0 copy-start.2
  87.8 0.0 copy-start.1
  87.8 2.8 %copy.16 = bf16[1,384,2048]{2,1,0:T(8,128)(2,1)} copy(bf16[1,384,2048]{2,1,0:T(8,128)(2,1)} %bitcast.10) | data formatting | bytes 3145728
  90.6 0.0 copy-done.2
  90.6 0.0 copy-start
  90.6 0.9 copy.17
  91.5 0.0 copy-done.1
  91.5 0.0 copy-start.3
  91.5 0.9 copy.18
  92.4 0.0 copy-done
  92.4 0.9 copy.19
  93.3 0.0 copy-done.3
  93.3 0.7 copy.20
Async XLA Ops:
  87.8 2.9 %copy-start.2 = (bf16[384,1024]{1,0:T(8,128)(2,1)S(1)}, bf16[384,1024]{1,0:T(8,128)(2,1)}, u32[]{:S(2)}) copy-start(bf16[384,1024]{1,0:T(8,128)(2,1)} %get-tuple-element.11) | copy-start | bytes 2359300
  87.8 3.7 %copy-start.1 = (bf16[384,1024]{1,0:T(8,128)(2,1)S(1)}, bf16[384,1024]{1,0:T(8,128)(2,1)}, u32[]{:S(2)}) copy-start(bf16[384,1024]{1,0:T(8,128)(2,1)} %get-tuple-element.12) | copy-start | bytes 2359300
  90.6 1.8 %copy-start = (bf16[384,1024]{1,0:T(8,128)(2,1)S(1)}, bf16[384,1024]{1,0:T(8,128)(2,1)}, u32[]{:S(2)}) copy-start(bf16[384,1024]{1,0:T(8,128)(2,1)} %get-tuple-element.13) | copy-start | bytes 2359300
  91.5 1.8 %copy-start.3 = (f32[64,1024]{1,0:T(8,128)S(1)}, f32[64,1024]{1,0:T(8,128)}, u32[]{:S(2)}) copy-start(f32[64,1024]{1,0:T(8,128)} %get-tuple-element.24) | copy-start | bytes 786436

commit v2 on v1

--- a/solution.py
+++ b/solution.py
@@ -13,7 +13,7 @@
 MESH = pl.DeviceIdType.MESH
 BF16 = jnp.bfloat16
 F32 = jnp.float32
-VMEM_BYTES = 60 * 1024 * 1024
+VMEM_BYTES = 52 * 1024 * 1024
 
 
 def mm(a, b, ca=1, cb=0):
@@ -394,7 +394,6 @@
         lax.fori_loop(0, n, body, 0)
 
     tile = 256
-    store = pltpu.make_async_copy(r["outv"], out, loc.at[1])
 
     def project():
         def body(i, carry):
@@ -402,11 +401,10 @@
             part = mm(seq[0], wv[0, at, :], 1, 1)
             for h in range(1, heads):
                 part += mm(seq[h], wv[h, at, :], 1, 1)
-            r["outv"][:, at] = part.astype(BF16)
+            out[:, at] = part.astype(BF16)
             return carry
 
         lax.fori_loop(0, model // tile, body, 0)
-        store.start()
 
     for h in range(heads):
         forward(h)
@@ -433,7 +431,17 @@
         trade.arrive()
     for trade in (*rows.values(), *cots, *attns, *grads.values()):
         trade.sent()
-    store.wait()
+
+
+def store_kernel(*refs):
+    sems = refs[-1]
+    copies = [
+        pltpu.make_async_copy(refs[i], refs[5 + i], sems.at[i]) for i in range(5)
+    ]
+    for copy in copies:
+        copy.start()
+    for copy in copies:
+        copy.wait()
 
 
 def shards(queries, keys, values, out_weight, out_cot, block_list):
@@ -461,7 +469,6 @@
         "octv": pltpu.VMEM((model, tokens), BF16),
         "wv": pltpu.VMEM((heads, model, width), BF16),
         "seq": pltpu.VMEM((heads, tokens, width), BF16),
-        "outv": pltpu.VMEM((tokens, model), BF16),
         "cotbuf": pltpu.VMEM((heads, n, held, BLOCK_TOKENS, HEAD_SIZE), BF16),
         "attn": pltpu.VMEM(byhead, BF16),
         "dq": pltpu.VMEM(byhead, BF16),
@@ -481,7 +488,7 @@
         "xsend": pltpu.VMEM(cross, BF16),
         "xrecv": pltpu.VMEM(cross, BF16),
         "pos": pltpu.SMEM((blocks, blocks), jnp.int32),
-        "loc": dma((2,)),
+        "loc": dma((1,)),
         "wsem": dma((heads, n)),
         "in_s": dma((heads, 4, n)),
         "in_r": dma((heads, 4, n)),
@@ -502,22 +509,30 @@
             scratch[f"{t}{h}"] = pltpu.VMEM((blocks, BLOCK_TOKENS, HEAD_SIZE), BF16)
     rows = [x.reshape(held, BLOCK_TOKENS, total) for x in (queries, keys, values)]
     bytoken = jax.ShapeDtypeStruct((tokens, total), BF16)
-    out, dq, dk, dv, wg = pl.pallas_call(
+    results = (
+        jax.ShapeDtypeStruct((tokens, model), BF16),
+        bytoken,
+        bytoken,
+        bytoken,
+        jax.ShapeDtypeStruct((sub, total), F32),
+    )
+    held_results = pl.pallas_call(
         functools.partial(layer_kernel, n, nz, heads, tuple(scratch)),
-        out_shape=(
-            jax.ShapeDtypeStruct((tokens, model), BF16),
-            bytoken,
-            bytoken,
-            bytoken,
-            jax.ShapeDtypeStruct((sub, total), F32),
-        ),
+        out_shape=tuple(pltpu.VMEM(x.shape, x.dtype) for x in results),
         in_specs=[sspec] + [anyspec] * 5,
-        out_specs=(anyspec, anyspec, anyspec, anyspec, vspec),
+        out_specs=(vspec,) * 5,
         scratch_shapes=list(scratch.values()),
         compiler_params=pltpu.CompilerParams(
             collective_id=0, has_side_effects=True, vmem_limit_bytes=VMEM_BYTES
         ),
     )(block_list.T, *rows, out_weight, out_cot[0])
+    out, dq, dk, dv, wg = pl.pallas_call(
+        store_kernel,
+        out_shape=results,
+        in_specs=[vspec] * 5,
+        out_specs=(anyspec,) * 5,
+        scratch_shapes=[dma((5,))], compiler_params=pltpu.CompilerParams(vmem_limit_bytes=1024 * 1024),
+    )(*[pltpu.with_memory_space_constraint(x, pltpu.VMEM) for x in held_results])
     return out[None], dq[None], dk[None], dv[None], wg
 
 

time: 95.2 us -> 90.3 us (0.949)
  local copies, waits for them, and re-layouts: 6.2 us -> 0 us
  Pallas kernels: 87.1 us -> 88.4 us
    unnamed x13 -> x0, local copies, waits for them, and re-layouts: 6.2 us -> none
    pallas_call x0 -> x1, Pallas kernels: none -> 2.04 us  [shards(): pl.pallas_call(store_kernel, out_shape=results, in_specs=[vspec] * 5, out...]
where the time goes in v2:
time: 90.3 us; the launch traced here: 89 us
  Pallas kernels  88.4 us (98%)
    pallas_call x1, Pallas kernels, shards(): pl.pallas_call(functools.partial(layer_kernel, n, nz, heads, tuple(scratc...  86.3 us
    pallas_call x1, Pallas kernels, shards(): pl.pallas_call(store_kernel, out_shape=results, in_specs=[vspec] * 5, out...  2.04 us

profile of v2, /device:TPU:8, one launch (start us, length us, event | category | flops | bytes accessed | tf_op | source)
XLA Modules:
  0.0 89.0 jit_solution(2465971357245827174)
XLA Ops:
  0.6 86.3 %shard_map.101 = (bf16[384,2048]{1,0:T(8,128)(2,1)S(1)}, bf16[384,1024]{1,0:T(8,128)(2,1)S(1)}, bf16[384,1024]{1,0:T(8,128)(2,1)S(1)}, bf16[384,1024]{1,0:T(8,128)(2,1)S(1)}, f32[64,1024]{1,0:T(8,128)S(1)}) custom-call(s32[8,12]{1,0:T(8,128)} %bitcast.13, bf16[3,128,1024]{2,1,0:T(8,128)(2,1)} %bitcast.10, bf16[3,128,1024]{2,1,0:T(8,128)(2,1)} %bitcast.11, ...), custom_call_target="tpu_custom_call" | custom-call | tf_op jit(solution)/shard_map/pallas_call | solution.py:519
  87.0 2.0 %shard_map.102 = (bf16[384,2048]{1,0:T(8,128)(2,1)}, bf16[384,1024]{1,0:T(8,128)(2,1)}, bf16[384,1024]{1,0:T(8,128)(2,1)}, bf16[384,1024]{1,0:T(8,128)(2,1)}, f32[64,1024]{1,0:T(8,128)}) custom-call(bf16[384,2048]{1,0:T(8,128)(2,1)S(1)} %get-tuple-element.15.refs_0_, bf16[384,1024]{1,0:T(8,128)(2,1)S(1)} %get-tuple-element.16.refs_1_, ...), custom_call_target="tpu_custom_call" | custom-call | tf_op jit(solution)/shard_map/pallas_call | solution.py:529

commit v3 on v2

--- a/solution.py
+++ b/solution.py
@@ -10,6 +10,7 @@
 
 HEAD_SIZE = 128
 BLOCK_TOKENS = 128
+EARLY = 2
 MESH = pl.DeviceIdType.MESH
 BF16 = jnp.bfloat16
 F32 = jnp.float32
@@ -50,9 +51,18 @@
         pl.semaphore_signal(
             barrier, inc=1, device_id=(dp, lax.rem(me + d, n)), device_id_type=MESH
         )
-    for target in (other, up, down):
-        pl.semaphore_signal(barrier, inc=1, device_id=(target, me), device_id_type=MESH)
-    pl.semaphore_wait(barrier, n - 1 + 3)
+    pl.semaphore_signal(barrier, inc=1, device_id=(other, me), device_id_type=MESH)
+
+    @pl.when(z < nz - 1)
+    def _():
+        pl.semaphore_signal(barrier, inc=1, device_id=(up, me), device_id_type=MESH)
+
+    @pl.when(z > 0)
+    def _():
+        pl.semaphore_signal(barrier, inc=1, device_id=(down, me), device_id_type=MESH)
+
+    ends = jnp.where(z == 0, 1, 0) + jnp.where(z == nz - 1, 1, 0)
+    pl.semaphore_wait(barrier, n - 1 + 3 - ends)
 
     def partner(d):
         return lax.rem(me + d, n)
@@ -115,9 +125,13 @@
         for h in range(heads)
     }
 
-    for h in range(heads):
-        for t in "kqv":
-            rows[t, h].start()
+    order = [rows[t, h] for h in range(heads) for t in "kqv"]
+
+    def send_rows(first, last):
+        for trade in order[first:last]:
+            trade.start()
+
+    send_rows(0, 3 + EARLY)
     load_oc = pltpu.make_async_copy(oc, ocv, loc.at[0])
     load_oc.start()
     load_w = []
@@ -173,16 +187,18 @@
     def listed(ref, i, axis):
         return jnp.concatenate([ref[picks[j, i]] for j in range(chosen)], axis=axis)
 
-    def forward_block(h, i):
+    def score_block(h, i):
         st = mm(listed(r[f"k{h}"], i, 0), r[f"q{h}"][i], 1, 1)
         top = jnp.max(st, axis=0, keepdims=True)
         e = jnp.exp2((st - top) * factor)
         inv = 1.0 / jnp.sum(e, axis=0, keepdims=True)
         low = (e * inv).astype(BF16)
+        ps[h, pl.ds(i * chosen, chosen)] = low.reshape(chosen, BLOCK_TOKENS, BLOCK_TOKENS)
+
+    def mix_block(h, i):
+        low = ps[h, pl.ds(i * chosen, chosen)].reshape(-1, BLOCK_TOKENS)
         a = mm(listed(vt, i, 1), low).astype(BF16)
         r["attn"][h, span(i, BLOCK_TOKENS), :] = a.T
-        for j in range(chosen):
-            ps[h, i * chosen + j] = low[j * BLOCK_TOKENS : (j + 1) * BLOCK_TOKENS]
 
     def backward_block(h, i):
         at = span(i, BLOCK_TOKENS)
@@ -240,14 +256,24 @@
         for trade in trades:
             trade.own().start()
 
-    def forward(h):
-        for t in "kqv":
+    def score(h):
+        for t in "kq":
             rows[t, h].arrive()
+
+        def body(p, carry):
+            for x in range(held):
+                score_block(h, p * held + x)
+            return carry
+
+        lax.fori_loop(0, n, body, 0)
+
+    def mix(h):
+        rows["v", h].arrive()
         turn(r[f"v{h}"], vt)
 
         def work(p):
             for x in range(held):
-                forward_block(h, p * held + x)
+                mix_block(h, p * held + x)
 
         by_partner(work, [attns[h]], {})
 
@@ -406,19 +432,44 @@
 
         lax.fori_loop(0, model // tile, body, 0)
 
-    for h in range(heads):
-        forward(h)
-        cots[h].start()
-    for h in range(heads):
-        attns[h].arrive()
-        give(h)
+    def begin(h):
         take(h)
         burst(h, 0)
-        hooks = {n // 2 - 1: lambda: burst(h, 1)}
-        if h > 0:
-            hooks[0] = lambda: finish(h - 1)
-        backward(h, hooks)
-        collect(h, {n // 2 - 1: lambda: burst(h, 2)})
+
+    half = n // 2 - 1
+    last = n - 1
+    score(0)
+    mix(0)
+    send_rows(3 + EARLY, 6 + EARLY)
+    for h in range(1, heads):
+        score(h)
+        attns[h - 1].arrive()
+        give(h - 1)
+        cots[h - 1].start()
+        mix(h)
+        send_rows(3 * h + 3 + EARLY, 3 * h + 6 + EARLY)
+        begin(h - 1)
+    cots[heads - 1].start()
+    for h in range(heads):
+        if h == heads - 1:
+            attns[h].arrive()
+            give(h)
+        if h == 0 and heads > 1:
+            backward(h, {half: lambda: burst(h, 1)})
+            burst(h, 2)
+        elif h == heads - 1:
+            hooks = {half: lambda: begin(h)}
+            if h > 0:
+                hooks[0] = lambda: finish(h - 1)
+            backward(h, hooks)
+            burst(h, 1)
+        else:
+            backward(h, {half: lambda: finish(h - 1), last: lambda: burst(h, 1)})
+            burst(h, 2)
+        if h == heads - 1:
+            collect(h, {half: lambda: burst(h, 2)})
+        else:
+            collect(h, {})
         for b in range(3, nz - 1):
             burst(h, b)
     project()

time: 90.3 us -> 86.6 us (0.959); the launches traced: 89 us -> 86.4 us
  Pallas kernels: 88.4 us -> 85.8 us
    pallas_call x1, Pallas kernels: 86.3 us -> 83.7 us  [shards(): pl.pallas_call(functools.partial(layer_kernel, n, nz, heads, tuple(scratc...]
where the time goes in v3:
time: 86.6 us; the launch traced here: 86.4 us
  Pallas kernels  85.8 us (99%)
    pallas_call x1, Pallas kernels, shards(): pl.pallas_call(functools.partial(layer_kernel, n, nz, heads, tuple(scratc...  83.7 us
    pallas_call x1, Pallas kernels, shards(): pl.pallas_call(store_kernel, out_shape=results, in_specs=[vspec] * 5, out...  2.04 us

profile of v3, /device:TPU:8, one launch (start us, length us, event | category | flops | bytes accessed | tf_op | source)
XLA Modules:
  0.0 86.4 jit_solution(4658719851296953057)
XLA Ops:
  0.6 83.7 %shard_map.101 = (bf16[384,2048]{1,0:T(8,128)(2,1)S(1)}, bf16[384,1024]{1,0:T(8,128)(2,1)S(1)}, bf16[384,1024]{1,0:T(8,128)(2,1)S(1)}, bf16[384,1024]{1,0:T(8,128)(2,1)S(1)}, f32[64,1024]{1,0:T(8,128)S(1)}) custom-call(s32[8,12]{1,0:T(8,128)} %bitcast.13, bf16[3,128,1024]{2,1,0:T(8,128)(2,1)} %bitcast.10, bf16[3,128,1024]{2,1,0:T(8,128)(2,1)} %bitcast.11, ...), custom_call_target="tpu_custom_call" | custom-call | tf_op jit(solution)/shard_map/pallas_call | solution.py:570
  84.4 2.0 %shard_map.102 = (bf16[384,2048]{1,0:T(8,128)(2,1)}, bf16[384,1024]{1,0:T(8,128)(2,1)}, bf16[384,1024]{1,0:T(8,128)(2,1)}, bf16[384,1024]{1,0:T(8,128)(2,1)}, f32[64,1024]{1,0:T(8,128)}) custom-call(bf16[384,2048]{1,0:T(8,128)(2,1)S(1)} %get-tuple-element.15.refs_0_, bf16[384,1024]{1,0:T(8,128)(2,1)S(1)} %get-tuple-element.16.refs_1_, ...), custom_call_target="tpu_custom_call" | custom-call | tf_op jit(solution)/shard_map/pallas_call | solution.py:580

commit v4 on v3

--- a/solution.py
+++ b/solution.py
@@ -455,18 +455,20 @@
             attns[h].arrive()
             give(h)
         if h == 0 and heads > 1:
-            backward(h, {half: lambda: burst(h, 1)})
-            burst(h, 2)
+            backward(h, {last: lambda: burst(h, 1)})
         elif h == heads - 1:
             hooks = {half: lambda: begin(h)}
             if h > 0:
-                hooks[0] = lambda: finish(h - 1)
+                hooks[last] = lambda: finish(h - 1)
             backward(h, hooks)
-            burst(h, 1)
+            if h == 0:
+                burst(h, 1)
         else:
             backward(h, {half: lambda: finish(h - 1), last: lambda: burst(h, 1)})
             burst(h, 2)
         if h == heads - 1:
+            collect(h, {0: lambda: burst(h, 1), last: lambda: burst(h, 2)} if h > 0 else {last: lambda: burst(h, 2)})
+        elif h == 0:
             collect(h, {half: lambda: burst(h, 2)})
         else:
             collect(h, {})

time: 86.6 us -> 85.3 us (0.985); the launches traced: 86.4 us -> 83.9 us
  Pallas kernels: 85.8 us -> 83.3 us
    pallas_call x1, Pallas kernels: 83.7 us -> 81.2 us  [shards(): pl.pallas_call(functools.partial(layer_kernel, n, nz, heads, tuple(scratc...]
where the time goes in v4:
time: 85.3 us; the launch traced here: 83.9 us
  Pallas kernels  83.3 us (98%)
    pallas_call x1, Pallas kernels, shards(): pl.pallas_call(functools.partial(layer_kernel, n, nz, heads, tuple(scratc...  81.2 us
    pallas_call x1, Pallas kernels, shards(): pl.pallas_call(store_kernel, out_shape=results, in_specs=[vspec] * 5, out...  2.04 us

profile of v4, /device:TPU:8, one launch (start us, length us, event | category | flops | bytes accessed | tf_op | source)
XLA Modules:
  0.0 83.9 jit_solution(2181694827896866562)
XLA Ops:
  0.6 81.2 %shard_map.101 = (bf16[384,2048]{1,0:T(8,128)(2,1)S(1)}, bf16[384,1024]{1,0:T(8,128)(2,1)S(1)}, bf16[384,1024]{1,0:T(8,128)(2,1)S(1)}, bf16[384,1024]{1,0:T(8,128)(2,1)S(1)}, f32[64,1024]{1,0:T(8,128)S(1)}) custom-call(s32[8,12]{1,0:T(8,128)} %bitcast.13, bf16[3,128,1024]{2,1,0:T(8,128)(2,1)} %bitcast.10, bf16[3,128,1024]{2,1,0:T(8,128)(2,1)} %bitcast.11, ...), custom_call_target="tpu_custom_call" | custom-call | tf_op jit(solution)/shard_map/pallas_call | solution.py:572
  81.9 2.0 %shard_map.102 = (bf16[384,2048]{1,0:T(8,128)(2,1)}, bf16[384,1024]{1,0:T(8,128)(2,1)}, bf16[384,1024]{1,0:T(8,128)(2,1)}, bf16[384,1024]{1,0:T(8,128)(2,1)}, f32[64,1024]{1,0:T(8,128)}) custom-call(bf16[384,2048]{1,0:T(8,128)(2,1)S(1)} %get-tuple-element.15.refs_0_, bf16[384,1024]{1,0:T(8,128)(2,1)S(1)} %get-tuple-element.16.refs_1_, ...), custom_call_target="tpu_custom_call" | custom-call | tf_op jit(solution)/shard_map/pallas_call | solution.py:582

commit v5 on v4

--- a/solution.py
+++ b/solution.py
@@ -451,13 +451,16 @@
         begin(h - 1)
     cots[heads - 1].start()
     for h in range(heads):
-        if h == heads - 1:
+        if h == 0 and heads == 1:
             attns[h].arrive()
             give(h)
         if h == 0 and heads > 1:
             backward(h, {last: lambda: burst(h, 1)})
+            if h == heads - 2:
+                attns[h + 1].arrive()
+                give(h + 1)
         elif h == heads - 1:
-            hooks = {half: lambda: begin(h)}
+            hooks = {0: lambda: begin(h)}
             if h > 0:
                 hooks[last] = lambda: finish(h - 1)
             backward(h, hooks)
@@ -466,15 +469,22 @@
         else:
             backward(h, {half: lambda: finish(h - 1), last: lambda: burst(h, 1)})
             burst(h, 2)
+            if h == heads - 2:
+                attns[h + 1].arrive()
+                give(h + 1)
         if h == heads - 1:
-            collect(h, {0: lambda: burst(h, 1), last: lambda: burst(h, 2)} if h > 0 else {last: lambda: burst(h, 2)})
+            collect(h, {half: lambda: burst(h, 1)} if h > 0 else {last: lambda: burst(h, 2)})
         elif h == 0:
             collect(h, {half: lambda: burst(h, 2)})
         else:
             collect(h, {})
         for b in range(3, nz - 1):
-            burst(h, b)
+            if h == 0 or h + 1 < heads:
+                burst(h, b)
     project()
+    if heads > 1:
+        for b in range(2, nz - 1):
+            burst(heads - 1, b)
     finish(heads - 1)
     for h in range(heads):
         total(h)

time: 85.3 us -> 85.2 us (level)
  no operation moved by 1% of the time
where the time goes in v5:
time: 85.2 us; the launch traced here: 83.6 us
  Pallas kernels  82.9 us (97%)
    pallas_call x1, Pallas kernels, shards(): pl.pallas_call(functools.partial(layer_kernel, n, nz, heads, tuple(scratc...  80.9 us
    pallas_call x1, Pallas kernels, shards(): pl.pallas_call(store_kernel, out_shape=results, in_specs=[vspec] * 5, out...  2.04 us

profile of v5, /device:TPU:8, one launch (start us, length us, event | category | flops | bytes accessed | tf_op | source)
XLA Modules:
  0.0 83.6 jit_solution(1019145607802885345)
XLA Ops:
  0.6 80.9 %shard_map.101 = (bf16[384,2048]{1,0:T(8,128)(2,1)S(1)}, bf16[384,1024]{1,0:T(8,128)(2,1)S(1)}, bf16[384,1024]{1,0:T(8,128)(2,1)S(1)}, bf16[384,1024]{1,0:T(8,128)(2,1)S(1)}, f32[64,1024]{1,0:T(8,128)S(1)}) custom-call(s32[8,12]{1,0:T(8,128)} %bitcast.13, bf16[3,128,1024]{2,1,0:T(8,128)(2,1)} %bitcast.10, bf16[3,128,1024]{2,1,0:T(8,128)(2,1)} %bitcast.11, ...), custom_call_target="tpu_custom_call" | custom-call | tf_op jit(solution)/shard_map/pallas_call | solution.py:582
  81.5 2.0 %shard_map.102 = (bf16[384,2048]{1,0:T(8,128)(2,1)}, bf16[384,1024]{1,0:T(8,128)(2,1)}, bf16[384,1024]{1,0:T(8,128)(2,1)}, bf16[384,1024]{1,0:T(8,128)(2,1)}, f32[64,1024]{1,0:T(8,128)}) custom-call(bf16[384,2048]{1,0:T(8,128)(2,1)S(1)} %get-tuple-element.15.refs_0_, bf16[384,1024]{1,0:T(8,128)(2,1)S(1)} %get-tuple-element.16.refs_1_, ...), custom_call_target="tpu_custom_call" | custom-call | tf_op jit(solution)/shard_map/pallas_call | solution.py:592

commit v6 on v5

--- a/solution.py
+++ b/solution.py
@@ -485,14 +485,17 @@
     if heads > 1:
         for b in range(2, nz - 1):
             burst(heads - 1, b)
+    for trade in (*rows.values(), *cots, *attns):
+        trade.sent()
+    for h in range(heads - 1):
+        total(h)
+        drain(h)
     finish(heads - 1)
-    for h in range(heads):
-        total(h)
-    for h in range(heads):
-        drain(h)
+    total(heads - 1)
+    drain(heads - 1)
     for trade in grads.values():
         trade.arrive()
-    for trade in (*rows.values(), *cots, *attns, *grads.values()):
+    for trade in grads.values():
         trade.sent()
 
 

time: 85.2 us -> 85.1 us (level)
  no operation moved by 1% of the time
where the time goes in v6:
time: 85.1 us; the launch traced here: 83.4 us
  Pallas kernels  82.8 us (97%)
    pallas_call x1, Pallas kernels, shards(): pl.pallas_call(functools.partial(layer_kernel, n, nz, heads, tuple(scratc...  80.8 us
    pallas_call x1, Pallas kernels, shards(): pl.pallas_call(store_kernel, out_shape=results, in_specs=[vspec] * 5, out...  2.04 us

profile of v6, /device:TPU:8, one launch (start us, length us, event | category | flops | bytes accessed | tf_op | source)
XLA Modules:
  0.0 83.4 jit_solution(8135311294531250801)
XLA Ops:
  0.6 80.8 %shard_map.101 = (bf16[384,2048]{1,0:T(8,128)(2,1)S(1)}, bf16[384,1024]{1,0:T(8,128)(2,1)S(1)}, bf16[384,1024]{1,0:T(8,128)(2,1)S(1)}, bf16[384,1024]{1,0:T(8,128)(2,1)S(1)}, f32[64,1024]{1,0:T(8,128)S(1)}) custom-call(s32[8,12]{1,0:T(8,128)} %bitcast.13, bf16[3,128,1024]{2,1,0:T(8,128)(2,1)} %bitcast.10, bf16[3,128,1024]{2,1,0:T(8,128)(2,1)} %bitcast.11, ...), custom_call_target="tpu_custom_call" | custom-call | tf_op jit(solution)/shard_map/pallas_call | solution.py:585
  81.4 2.0 %shard_map.102 = (bf16[384,2048]{1,0:T(8,128)(2,1)}, bf16[384,1024]{1,0:T(8,128)(2,1)}, bf16[384,1024]{1,0:T(8,128)(2,1)}, bf16[384,1024]{1,0:T(8,128)(2,1)}, f32[64,1024]{1,0:T(8,128)}) custom-call(bf16[384,2048]{1,0:T(8,128)(2,1)S(1)} %get-tuple-element.15.refs_0_, bf16[384,1024]{1,0:T(8,128)(2,1)S(1)} %get-tuple-element.16.refs_1_, ...), custom_call_target="tpu_custom_call" | custom-call | tf_op jit(solution)/shard_map/pallas_call | solution.py:595
